TPU v7x, 32 devices: a whole 2x2x4 slice. The times are simulated.
32 devices in a mesh: groups: 2 (over y), seq: 8 (over z, x), head: 2 (over core).
Axes of the slice: x: 2, y: 2, z: 4, core: 2. Of those that a mesh axis runs over, the one named last changes fastest.
Arguments:
- text_query_rows: bfloat16 [2048, 8192], P(('groups', 'seq'), 'head'), parts along dimension 0, may hold values from -40 to 40, as said below
- text_key_value: bfloat16 [2, 2048, 1024], P(None, ('groups', 'seq'), 'head'), parts along dimension 1, may hold values from -4 to 4, as said below
- doc_ids: int32 [2048], P(('groups', 'seq')), parts along dimension 0, may hold values from 0 to 3, never falling along the last dimension, each value on 1 to 512 neighbouring positions
- tile_span: int32 [2048, 2], P(('groups', 'seq')), parts along dimension 0, may hold values from 0 to 8, as said below
- vision_hidden: bfloat16 [4096, 1280], P(('groups', 'seq')), parts along dimension 0, may hold values from -6 to 6
- vision_qkv: bfloat16 [3, 4096, 1280], P(None, ('groups', 'seq'), 'head'), parts along dimension 1, may hold values from -6 to 6, as said below
- vision_out_weight: bfloat16 [1280, 1280], P('head'), may hold values from -0.625 to 0.625
- cross_keyvalue_weight: bfloat16 [1280, 2, 1024], P('seq', None, 'head'), may hold values from -0.15625 to 0.15625
- cross_gate: float32 [64], P('head'), may hold values from -1.5 to 1.5
Outputs:
- attention_out: bfloat16 [2048, 8192], P(('groups', 'seq'), 'head'), parts along dimension 0
There are 2 independent parts, one for each index of `groups`. A program takes and returns all parts, laid end to end along the dimension named above; an argument that names none is the same for every part. Nothing has to cross between parts.
Inputs may be any that keep to these rules, and one draw needn't show every extreme that they name: `tile_span`: each text token's span is an interval of the tiles of its own block b = p // 128 and of block b - 1 (first <= second, both between b - 1 and b + 1, never below 0); it may be empty. `doc_ids`: never falling along the document; each segment holds 1 to 512 tokens. `text_query_rows`: real values. `text_key_value`: real values. `vision_qkv`: real values.
All inputs are finite; a program needn't handle non-finite values.
Results may differ from a plain program's by a relative error of at most 0.024.
Values may be sent and summed in bfloat16 or wider, within the bound.
A program may use at most 64 MiB of HBM per device.

v0:
```python
import math
import jax
import jax.numpy as jnp
from jax import lax
from jax.sharding import PartitionSpec as P

HEAD_SIZE = 128
VHD = 80
WINDOW_BLOCKS = 2


def passed_along(block, axis, distance):
    devices = range(lax.axis_size(axis))
    route = [(i - distance, i) for i in devices if i - distance in devices]
    return lax.ppermute(block, axis, route)


def attend_heads(query_rows, keys, allowed_mask):
    scores = jnp.einsum(
        "tgrd,kgd->grtk", query_rows, keys, preferred_element_type=jnp.float32
    ) / math.sqrt(HEAD_SIZE)
    scores = jnp.where(allowed_mask[None, None], scores, -1e30)
    return jax.nn.softmax(scores, axis=-1)


def per_device(
    text_query_rows,
    text_key_value,
    doc_ids,
    tile_span,
    vision_hidden,
    vision_qkv,
    vision_out_weight,
    cross_keyvalue_weight,
    cross_gate,
):
    text_rows = text_query_rows.shape[0]
    tile_rows = vision_hidden.shape[0]
    kv_cols = text_key_value.shape[2]
    kv_heads = kv_cols // HEAD_SIZE
    query_group_ratio = text_query_rows.shape[1] // HEAD_SIZE // kv_heads
    seq_index = lax.axis_index("seq")
    vision_query = vision_qkv[0].reshape(tile_rows, -1, VHD)
    vision_key = vision_qkv[1].reshape(tile_rows, -1, VHD)
    vision_value = vision_qkv[2].reshape(tile_rows, -1, VHD)
    vision_scores = jnp.einsum(
        "qhd,khd->hqk", vision_query, vision_key, preferred_element_type=jnp.float32
    ) / math.sqrt(VHD)
    vision_weights = jax.nn.softmax(vision_scores, axis=-1).astype(jnp.bfloat16)
    vision_attn = jnp.einsum(
        "hqk,khd->qhd", vision_weights, vision_value, preferred_element_type=jnp.float32
    )
    vision_attn = vision_attn.astype(jnp.bfloat16).reshape(tile_rows, -1)
    partial_mix = jnp.dot(vision_attn, vision_out_weight, preferred_element_type=jnp.float32)
    mixed_sum = lax.psum(partial_mix, "head") + vision_hidden.astype(jnp.float32)
    image_norm = (
        mixed_sum * lax.rsqrt(jnp.mean(mixed_sum * mixed_sum, axis=-1, keepdims=True) + 1e-05)
    ).astype(jnp.bfloat16)
    image_key_value = jnp.einsum(
        "ic,cjf->ijf",
        image_norm,
        lax.all_gather(cross_keyvalue_weight, "seq", axis=0, tiled=True),
        preferred_element_type=jnp.float32,
    ).astype(jnp.bfloat16)
    earlier_tile = passed_along(image_key_value, "seq", 1)
    blocks = [(text_key_value, doc_ids)]
    current_kv, current_docs = (text_key_value, doc_ids)
    for repeat_count in range(WINDOW_BLOCKS):
        current_kv, current_docs = passed_along((current_kv, current_docs), "seq", 1)
        blocks.insert(0, (current_kv, current_docs))
    all_keyval = jnp.concatenate([member[0] for member in blocks], axis=1)
    all_docs = jnp.concatenate([member[1] for member in blocks], axis=0)
    key_pos = (seq_index - WINDOW_BLOCKS) * text_rows + jnp.arange(
        (WINDOW_BLOCKS + 1) * text_rows, dtype=jnp.int32
    )
    query_pos = seq_index * text_rows + jnp.arange(text_rows, dtype=jnp.int32)
    allowed_mask = (
        (all_docs[None, :] == doc_ids[:, None])
        & (key_pos[None, :] <= query_pos[:, None])
        & (key_pos[None, :] >= 0)
    )
    query_rows = text_query_rows.reshape(text_rows, kv_heads, query_group_ratio, HEAD_SIZE)
    self_attention_weights = attend_heads(
        query_rows, all_keyval[0].reshape(-1, kv_heads, HEAD_SIZE), allowed_mask
    ).astype(jnp.bfloat16)
    self_output = jnp.einsum(
        "ycmq,qyb->mycb",
        self_attention_weights,
        all_keyval[1].reshape(-1, kv_heads, HEAD_SIZE),
        preferred_element_type=jnp.float32,
    )
    self_output = self_output.reshape(text_rows, -1)
    image_all = jnp.concatenate([earlier_tile, image_key_value], axis=0)
    tile_ids = seq_index - 1 + jnp.arange(2 * tile_rows, dtype=jnp.int32) // tile_rows
    low_tile = tile_span[:, 0]
    high_tile = tile_span[:, 1]
    visible_mask = (tile_ids[None, :] >= low_tile[:, None]) & (
        tile_ids[None, :] < high_tile[:, None]
    )
    image_present = (high_tile > low_tile).astype(jnp.float32)
    cross_probabilities = (
        attend_heads(query_rows, image_all[:, 0].reshape(-1, kv_heads, HEAD_SIZE), visible_mask)
        * image_present[None, None, :, None]
    )
    cross_probabilities = cross_probabilities.astype(jnp.bfloat16)
    cross_output = jnp.einsum(
        "ycmq,qyb->mycb",
        cross_probabilities,
        image_all[:, 1].reshape(-1, kv_heads, HEAD_SIZE),
        preferred_element_type=jnp.float32,
    )
    cross_output = cross_output.reshape(text_rows, -1)
    gate_cols = jnp.repeat(jnp.tanh(cross_gate), HEAD_SIZE)
    return (self_output + gate_cols[None, :] * cross_output).astype(jnp.bfloat16)


def solution(mesh):
    placed = (
        P(("groups", "seq"), "head"),
        P(None, ("groups", "seq"), "head"),
        P(("groups", "seq")),
        P(("groups", "seq"), None),
        P(("groups", "seq"), None),
        P(None, ("groups", "seq"), "head"),
        P("head", None),
        P("seq", None, "head"),
        P("head"),
    )
    return jax.shard_map(
        per_device,
        mesh=mesh,
        in_specs=placed,
        out_specs=P(("groups", "seq"), "head"),
        check_vma=False,
    )
```

profile of v0, /device:TPU:8, one launch (start us, length us, event | category | flops | bytes accessed | tf_op | source)
XLA Modules:
  0.0 130.6 jit_solution(16018390959418832903)
XLA Ops:
  7.4 1.4 %fusion.35 = (bf16[1,256,640]{2,1,0:T(8,128)(2,1)S(1)}, bf16[1,256,640]{2,1,0:T(8,128)(2,1)S(1)}, bf16[1,256,640]{2,1,0:T(8,128)(2,1)S(1)}) fusion(bf16[3,256,640]{2,1,0:T(8,128)(2,1)} %param.14), kind=kLoop, calls=%fused_computation.67 | loop fusion | bytes 1966080 | tf_op jit(solution)/shard_map/slice | solution.py:44
  8.8 0.2 copy.30
  8.9 0.2 copy.29
  9.1 0.2 copy.31
  9.3 2.2 %fusion.38 = (f32[8,256]{1,0:T(8,128)S(1)}, f32[8,256,256]{1,2,0:T(8,128)}) fusion(bf16[256,8,80]{0,2,1:T(8,128)(2,1)S(1)} %bitcast.88, bf16[256,8,80]{0,2,1:T(8,128)(2,1)S(1)} %bitcast.87), kind=kOutput, calls=%fused_computation.70 | convolution fusion | flops 85459200 | bytes 2760704 | tf_op jit(solution)/shard_map/sub | solution.py:49
  11.5 1.9 %convolution_convert_fusion.1 = bf16[8,256,80]{1,2,0:T(8,128)(2,1)S(1)} fusion(bf16[256,8,80]{0,2,1:T(8,128)(2,1)S(1)} %bitcast.89, f32[8,256,256]{1,2,0:T(8,128)} %get-tuple-element.17, f32[8,256]{1,0:T(8,128)S(1)} %get-tuple-element.16), kind=kOutput, calls=%fused_computation.28 | convolution fusion | flops 85098496 | bytes 2760704 | tf_op jit(solution)/shard_map/hqk,khd->qhd/dot_general | solution.py:50
  13.4 0.0 copy-start.5
  13.4 0.0 copy-start.4
  13.4 0.0 copy-start.7
  13.4 0.0 copy-start.6
  13.4 1.8 %fusion.40 = f32[256,1280]{1,0:T(8,128)} fusion(bf16[256,640]{0,1:T(8,128)(2,1)S(1)} %bitcast.86, bf16[640,1280]{1,0:T(8,128)(2,1)S(1)} %copy-done), kind=kOutput, calls=%fused_computation.72 | convolution fusion | flops 419430400 | bytes 3276800 | tf_op jit(solution)/shard_map/dot_general | solution.py:54
  15.2 0.0 all-reduce.2.cloned.1.call-update
  15.2 0.0 all-gather.2.cloned.1.call-start
  15.3 0.8 copy.33
  16.1 0.0 all-gather.2.cloned.1.call-update
  16.1 3.4 %collective-permute-start.2 = (s32[128]{0:T(128)S(1)}, s32[128]{0:T(128)S(1)}, u32[]{:S(2)}, u32[]{:S(2)}) collective-permute-start(s32[128]{0:T(128)S(1)} %copy-done.5), channel_id=1, source_target_pairs={{0,2},{2,4},{4,6},{6,8},{8,10},{10,12},{12,14},{1,3},{3,5},{5,7},{... | collective-permute-start | bytes 1544 | tf_op jit(solution)/shard_map/ppermute | solution.py:15
  19.5 0.2 copy.24
  19.7 3.5 %collective-permute-start = (bf16[2,128,512]{1,2,0:T(8,128)(2,1)S(1)}, bf16[2,128,512]{1,2,0:T(8,128)(2,1)S(1)}, u32[]{:S(2)}, u32[]{:S(2)}) collective-permute-start(bf16[2,128,512]{1,2,0:T(8,128)(2,1)S(1)} %copy.24), channel_id=1, source_target_pairs={{0,2},{2,4},{4,6},{6,8},{8,10},{10,12},{12,14},{1,3},{3,5},{5,7},{... | collective-permute-start | bytes 786440 | tf_op jit(solution)/shard_map/ppermute | solution.py:15
  23.2 0.1 broadcast_bitcast_fusion
  23.3 0.1 compare_and_fusion
  23.5 0.0 collective-permute-done.2
  23.5 3.4 %collective-permute-start.3 = (s32[128]{0:T(128)S(1)}, s32[128]{0:T(128)S(1)}, u32[]{:S(2)}, u32[]{:S(2)}) collective-permute-start(s32[128]{0:T(128)S(1)} %collective-permute-done.2), channel_id=1, source_target_pairs={{0,2},{2,4},{4,6},{6,8},{8,10},{10,12},{12,14},{1,3},{3,5},{5,7},{... | collective-permute-start | bytes 1544 | tf_op jit(solution)/shard_map/ppermute | solution.py:15
  26.9 1.5 %copy.52 = bf16[16,8,32,128]{3,2,1,0:T(8,128)(2,1)S(1)} copy(bf16[16,8,32,128]{3,1,2,0:T(8,128)(2,1)} %bitcast.83) | data formatting | bytes 2097152
  28.4 2.6 %collective-permute-done = bf16[2,128,512]{1,2,0:T(8,128)(2,1)S(1)} collective-permute-done((bf16[2,128,512]{1,2,0:T(8,128)(2,1)S(1)}, bf16[2,128,512]{1,2,0:T(8,128)(2,1)S(1)}, u32[]{:S(2)}, u32[]{:S(2)}) %collective-permute-start) | collective-permute-done | bytes 262176 | tf_op jit(solution)/shard_map/ppermute | solution.py:15
  30.9 3.1 %collective-permute-start.1 = (bf16[2,128,512]{1,2,0:T(8,128)(2,1)S(1)}, bf16[2,128,512]{1,2,0:T(8,128)(2,1)S(1)}, u32[]{:S(2)}, u32[]{:S(2)}) collective-permute-start(bf16[2,128,512]{1,2,0:T(8,128)(2,1)S(1)} %collective-permute-done), channel_id=1, source_target_pairs={{0,2},{2,4},{4,6},{6,8},{8,10},{10,12},{12,14},{1,3},{3,5},{5,7},{... | collective-permute-start | bytes 786440 | tf_op jit(solution)/shard_map/ppermute | solution.py:15
  34.0 0.0 collective-permute-done.3
  34.0 0.2 and_and_fusion
  34.2 12.1 %collective-permute-done.1 = bf16[2,128,512]{1,2,0:T(8,128)(2,1)S(1)} collective-permute-done((bf16[2,128,512]{1,2,0:T(8,128)(2,1)S(1)}, bf16[2,128,512]{1,2,0:T(8,128)(2,1)S(1)}, u32[]{:S(2)}, u32[]{:S(2)}) %collective-permute-start.1) | collective-permute-done | bytes 262176 | tf_op jit(solution)/shard_map/ppermute | solution.py:15
  46.4 0.1 pad_maximum_fusion
  46.5 0.8 fusion.36
  47.3 1.0 fusion.17
  48.4 0.0 copy-start.1
  48.4 3.7 %fusion.37 = (f32[4,8,128]{2,1,0:T(8,128)S(1)}, f32[4,8,128,384]{2,3,1,0:T(8,128)}) fusion(f32[4,384,128,8]{2,1,3,0:T(8,128)S(1)} %fusion.17, pred[128,384]{0,1:T(8,128)(4,1)S(1)} %and_and_fusion), kind=kOutput, calls=%fused_computation.69 | output fusion | flops 9437567 | bytes 12648448 | tf_op jit(solution)/shard_map/sub | solution.py:23
  52.1 1.6 %multiply_reduce_fusion.1 = f32[256]{0:T(256)S(1)} fusion(f32[256,1280]{1,0:T(8,128)} %all-reduce.2.cloned.1.call-done, bf16[256,1280]{1,0:T(8,128)(2,1)S(1)} %copy-done.1), kind=kLoop, calls=%fused_computation.25 | loop fusion | flops 1310464 | bytes 1967104 | tf_op jit(solution)/shard_map/reduce_sum | solution.py:57
  53.7 23.4 %all-gather.2.cloned.1.call-done = bf16[1280,2,512]{2,0,1:T(8,128)(2,1)} async-done(((bf16[160,2,512]{2,0,1:T(8,128)(2,1)}), bf16[1280,2,512]{2,0,1:T(8,128)(2,1)}) %all-gather.2.cloned.1.call-update) | async-done | bytes 2621456 | tf_op jit(solution)/shard_map/all_gather | solution.py:62
  77.1 3.9 %convolution_convert_fusion = bf16[256,2,512]{2,0,1:T(8,128)(2,1)} fusion(bf16[1280,2,512]{2,0,1:T(8,128)(2,1)} %all-gather.2.cloned.1.call-done, f32[256,1280]{1,0:T(8,128)} %all-reduce.2.cloned.1.call-done, bf16[256,1280]{1,0:T(8,128)(2,1)S(1)} %copy-done.1, f32[256]{0:T(256)S(1)} %add_rsqrt_fusion), kind=kOutput, calls=%fused_computation.27 | convolution fusion | flops 672661504 | bytes 5112832 | tf_op jit(solution)/shard_map/ic,cjf->ijf/dot_general | solution.py:59
  81.0 2.6 %collective-permute-start.4 = (bf16[256,2,512]{2,0,1:T(8,128)(2,1)}, bf16[256,2,512]{2,0,1:T(8,128)(2,1)S(1)}, u32[]{:S(2)}, u32[]{:S(2)}) collective-permute-start(bf16[256,2,512]{2,0,1:T(8,128)(2,1)} %convolution_convert_fusion), channel_id=1, source_target_pairs={{0,2},{2,4},{4,6},{6,8},{8,10},{10,12},{12,14},{1,3},{3,5},{5,7},{... | collective-permute-start | bytes 1572872 | tf_op jit(solution)/shard_map/ppermute | solution.py:15
  83.6 4.9 %fusion.11 = f32[4,128,8,128]{3,1,2,0:T(8,128)} fusion(bf16[384,4,128,1]{0,2,3,1:T(8,128)(2,1)S(1)} %bitcast.85, f32[4,8,128,384]{2,3,1,0:T(8,128)} %get-tuple-element.15, f32[4,8,128]{2,1,0:T(8,128)S(1)} %get-tuple-element.14), kind=kOutput, calls=%fused_computation.17 | convolution fusion | flops 405798912 | bytes 8798208 | tf_op jit(solution)/shard_map/ycmq,qyb->mycb/dot_general | solution.py:86
  88.5 2.9 %copy.39 = f32[128,4096]{1,0:T(8,128)} copy(f32[128,4096]{0,1:T(8,128)} %bitcast.81) | data formatting | bytes 4194304 | tf_op jit(solution)/shard_map/reshape | solution.py:92
  91.5 5.0 %collective-permute-done.4 = bf16[256,2,512]{2,0,1:T(8,128)(2,1)S(1)} collective-permute-done((bf16[256,2,512]{2,0,1:T(8,128)(2,1)}, bf16[256,2,512]{2,0,1:T(8,128)(2,1)S(1)}, u32[]{:S(2)}, u32[]{:S(2)}) %collective-permute-start.4) | collective-permute-done | bytes 524320 | tf_op jit(solution)/shard_map/ppermute | solution.py:15
  96.5 2.1 %pad_maximum_fusion.1 = (bf16[512,1,512]{2,0,1:T(8,128)(2,1)}, bf16[512,1,512]{2,0,1:T(8,128)(2,1)}) fusion(bf16[256,2,512]{2,0,1:T(8,128)(2,1)} %convolution_convert_fusion, bf16[256,2,512]{2,0,1:T(8,128)(2,1)S(1)} %collective-permute-done.4), kind=kLoop, calls=%fused_computation.40 | loop fusion | flops 2097152 | bytes 2097152 | tf_op jit(solution)/shard_map/concatenate | solution.py:93
  98.6 1.2 reshape_squeeze.27
  99.8 4.5 %fusion.15 = f32[4,512,128,8]{2,1,3,0:T(8,128)} fusion(bf16[128,4,8,128]{3,2,1,0:T(8,128)(2,1)S(1)} %bitcast.78, bf16[512,4,128,1]{2,1,0,3:T(4,128)(2,1)S(1)} %bitcast.79), kind=kOutput, calls=%fused_computation.32 | convolution fusion | flops 536870912 | bytes 9961472 | tf_op jit(solution)/shard_map/tgrd,kgd->grtk/dot_general | solution.py:19
  104.3 1.3 copy.49
  105.5 8.9 %fusion.39 = (f32[4,8,128]{2,1,0:T(8,128)S(1)}, f32[4,8,128,512]{2,3,1,0:T(8,128)S(1)}) fusion(f32[4,512,128,8]{2,1,3,0:T(8,128)} %fusion.15, pred[128,512]{0,1:T(8,128)(4,1)S(1)} %compare_and_fusion), kind=kOutput, calls=%fused_computation.71 | output fusion | flops 12583423 | bytes 16859136 | tf_op jit(solution)/shard_map/sub | solution.py:23
  114.4 2.3 %fusion.8 = f32[4,128,8,128]{3,1,2,0:T(8,128)} fusion(bf16[512,4,128,1]{0,2,3,1:T(8,128)(2,1)S(1)} %bitcast.84, f32[4,8,128,512]{2,3,1,0:T(8,128)S(1)} %get-tuple-element.19, f32[128]{0:T(128)S(1)} %compare_convert_fusion, f32[4,8,128]{2,1,0:T(8,128)S(1)} %get-tuple-element.18), kind=kOutput, calls=%fused_computation.14 | convolution fusion | flops 543162368 | bytes 11026944 | tf_op jit(solution)/shard_map/ycmq,qyb->mycb/dot_general | solution.py:106
  116.8 2.9 %copy.38 = f32[128,4096]{1,0:T(8,128)} copy(f32[128,4096]{0,1:T(8,128)} %bitcast.80) | data formatting | bytes 4194304 | tf_op jit(solution)/shard_map/reshape | solution.py:112
  119.7 3.5 %add_convert_fusion = bf16[128,4096]{1,0:T(8,128)(2,1)} fusion(f32[128,4096]{1,0:T(8,128)} %copy.39, f32[128,4096]{1,0:T(8,128)} %copy.38, f32[4096]{0:T(1024)S(1)} %broadcast_bitcast_fusion), kind=kLoop, calls=%fused_computation.19 | loop fusion | flops 1572864 | bytes 5259264 | tf_op jit(solution)/shard_map/convert_element_type | solution.py:114
  (22 shorter events, 0.1 us)
Async XLA Ops:
  7.4 6.0 %copy-start = (bf16[640,1280]{1,0:T(8,128)(2,1)S(1)}, bf16[640,1280]{1,0:T(8,128)(2,1)}, u32[]{:S(2)}) copy-start(bf16[640,1280]{1,0:T(8,128)(2,1)} %param.15) | copy-start | bytes 4915204
  7.4 44.7 %all-reduce.2.cloned.1.call-start = ((), (), s32[]{:S(2)}) async-start(), calls=%async_computation | async-start | bytes 2621440 | tf_op jit(solution)/shard_map/psum | solution.py:55
  13.4 1.9 %copy-start.3 = (bf16[160,2,512]{2,1,0:T(2,128)(2,1)S(1)}, bf16[160,2,512]{2,1,0:T(2,128)(2,1)}, u32[]{:S(2)}) copy-start(bf16[160,2,512]{2,1,0:T(2,128)(2,1)} %param.16) | copy-start | bytes 983044
  13.4 2.7 %copy-start.5 = (s32[128]{0:T(128)S(1)}, s32[128]{0:T(128)}, u32[]{:S(2)}) copy-start(s32[128]{0:T(128)} %param.11) | copy-start | bytes 1540
  13.4 6.1 %copy-start.4 = (bf16[2,128,512]{2,1,0:T(8,128)(2,1)S(1)}, bf16[2,128,512]{2,1,0:T(8,128)(2,1)}, u32[]{:S(2)}) copy-start(bf16[2,128,512]{2,1,0:T(8,128)(2,1)} %param.10) | copy-start | bytes 786436
  13.4 9.7 %copy-start.7 = (f32[32]{0:T(128)S(1)}, f32[32]{0:T(128)}, u32[]{:S(2)}) copy-start(f32[32]{0:T(128)} %param.17) | copy-start | bytes 388
  13.4 9.8 %copy-start.6 = (s32[128,2]{0,1:T(2,128)S(1)}, s32[128,2]{0,1:T(2,128)}, u32[]{:S(2)}) copy-start(s32[128,2]{0,1:T(2,128)} %param.12) | copy-start | bytes 3076
  15.2 61.9 %all-gather.2.cloned.1.call-start = ((), (), s32[]{:S(2)}) async-start(), calls=%async_computation.1 | async-start | bytes 2949120 | tf_op jit(solution)/shard_map/all_gather | solution.py:62
  16.1 7.4 %collective-permute-start.2 = (s32[128]{0:T(128)S(1)}, s32[128]{0:T(128)S(1)}, u32[]{:S(2)}, u32[]{:S(2)}) collective-permute-start(s32[128]{0:T(128)S(1)} %copy-done.5), channel_id=1, source_target_pairs={{0,2},{2,4},{4,6},{6,8},{8,10},{10,12},{12,14},{1,3},{3,5},{5,7},{... | collective-permute-start | bytes 1544 | tf_op jit(solution)/shard_map/ppermute | solution.py:15
  19.7 11.3 %collective-permute-start = (bf16[2,128,512]{1,2,0:T(8,128)(2,1)S(1)}, bf16[2,128,512]{1,2,0:T(8,128)(2,1)S(1)}, u32[]{:S(2)}, u32[]{:S(2)}) collective-permute-start(bf16[2,128,512]{1,2,0:T(8,128)(2,1)S(1)} %copy.24), channel_id=1, source_target_pairs={{0,2},{2,4},{4,6},{6,8},{8,10},{10,12},{12,14},{1,3},{3,5},{5,7},{... | collective-permute-start | bytes 786440 | tf_op jit(solution)/shard_map/ppermute | solution.py:15
  23.5 10.5 %collective-permute-start.3 = (s32[128]{0:T(128)S(1)}, s32[128]{0:T(128)S(1)}, u32[]{:S(2)}, u32[]{:S(2)}) collective-permute-start(s32[128]{0:T(128)S(1)} %collective-permute-done.2), channel_id=1, source_target_pairs={{0,2},{2,4},{4,6},{6,8},{8,10},{10,12},{12,14},{1,3},{3,5},{5,7},{... | collective-permute-start | bytes 1544 | tf_op jit(solution)/shard_map/ppermute | solution.py:15
  30.9 15.5 %collective-permute-start.1 = (bf16[2,128,512]{1,2,0:T(8,128)(2,1)S(1)}, bf16[2,128,512]{1,2,0:T(8,128)(2,1)S(1)}, u32[]{:S(2)}, u32[]{:S(2)}) collective-permute-start(bf16[2,128,512]{1,2,0:T(8,128)(2,1)S(1)} %collective-permute-done), channel_id=1, source_target_pairs={{0,2},{2,4},{4,6},{6,8},{8,10},{10,12},{12,14},{1,3},{3,5},{5,7},{... | collective-permute-start | bytes 786440 | tf_op jit(solution)/shard_map/ppermute | solution.py:15
  48.4 3.7 %copy-start.1 = (bf16[256,1280]{1,0:T(8,128)(2,1)S(1)}, bf16[256,1280]{1,0:T(8,128)(2,1)}, u32[]{:S(2)}) copy-start(bf16[256,1280]{1,0:T(8,128)(2,1)} %param.13) | copy-start | bytes 1966084
  77.1 6.5 %copy-start.2 = (bf16[1,384,512]{1,2,0:T(8,128)(2,1)S(1)}, bf16[1,384,512]{1,2,0:T(8,128)(2,1)}, u32[]{:S(2)}) copy-start(bf16[1,384,512]{1,2,0:T(8,128)(2,1)} %get-tuple-element.11) | copy-start | bytes 1179652
  81.0 15.5 %collective-permute-start.4 = (bf16[256,2,512]{2,0,1:T(8,128)(2,1)}, bf16[256,2,512]{2,0,1:T(8,128)(2,1)S(1)}, u32[]{:S(2)}, u32[]{:S(2)}) collective-permute-start(bf16[256,2,512]{2,0,1:T(8,128)(2,1)} %convolution_convert_fusion), channel_id=1, source_target_pairs={{0,2},{2,4},{4,6},{6,8},{8,10},{10,12},{12,14},{1,3},{3,5},{5,7},{... | collective-permute-start | bytes 1572872 | tf_op jit(solution)/shard_map/ppermute | solution.py:15
Sparse Core Ops, SparseCore 0:
  15.3 21.4 all-reduce.1
Sparse Core Ops, SparseCore 1:
  17.9 59.1 all-gather.1
where the time goes:
time: 131 us
  waiting for transfers between devices  43.2 us (33%)
  matrix products  22.5 us (17%)
  other arithmetic  20.2 us (15%)
  starting transfers between devices  16 us (12%)
  between operations  15.1 us (12%)
  local copies, waits for them, and re-layouts  13.6 us (10%)
    all_gather x1, waiting for transfers between devices, per_device(): lax.all_gather(cross_keyvalue_weight, 'seq', axis=0, tiled=True)  23.4 us
    ppermute x5, waiting for transfers between devices, passed_along(): return lax.ppermute(block, axis, route)  19.7 us
    ppermute x5, starting transfers between devices, passed_along(): return lax.ppermute(block, axis, route)  16 us
    sub x2, other arithmetic, attend_heads(): return jax.nn.softmax(scores, axis=-1)  12.6 us
    dot_general x2, matrix products, attend_heads(): jnp.einsum('tgrd,kgd->grtk', query_rows, keys, preferred_element_type=jnp...  5.54 us
    dot_general x1, matrix products, per_device(): jnp.einsum('ycmq,qyb->mycb', self_attention_weights, all_keyval[1].reshap...  4.89 us
    dot_general x1, matrix products, per_device(): jnp.einsum('ic,cjf->ijf', image_norm, lax.all_gather(cross_keyvalue_weigh...  3.87 us
    convert_element_type x1, other arithmetic, per_device(): (self_output + gate_cols[None, :] * cross_output).astype(jnp.bfloat16)  3.46 us
  transfers between devices with their start and end apart: 7, of which 4 were waited for; matrix products, arithmetic and copies ran while one was open for 14% of the time, Pallas kernels for 0%

commit v1 on v0

--- a/solution.py
+++ b/solution.py
@@ -56,11 +56,34 @@
     image_norm = (
         mixed_sum * lax.rsqrt(jnp.mean(mixed_sum * mixed_sum, axis=-1, keepdims=True) + 1e-05)
     ).astype(jnp.bfloat16)
-    image_key_value = jnp.einsum(
-        "ic,cjf->ijf",
-        image_norm,
-        lax.all_gather(cross_keyvalue_weight, "seq", axis=0, tiled=True),
-        preferred_element_type=jnp.float32,
+
+    def _state_wall(s0, incoming_x):
+        aux = lax.axis_size("seq")
+        local_out = lax.axis_index("seq")
+        e_now, r2, prior = (aux, local_out, s0.shape[0])
+        nodes = [(idx, (idx + 1) % e_now) for idx in range(e_now)]
+        tray = [(idx, (idx - 1) % e_now) for idx in range(e_now)]
+        back = e_now // 2
+        w2 = x_new = s0
+        main = incoming_x(s0, r2 * prior)
+        for h in range(1, back + 1):
+            w2 = lax.ppermute(w2, "seq", nodes)
+            if h < e_now - back:
+                x_new = lax.ppermute(x_new, axis_name="seq", perm=tray)
+                later = incoming_x(x_new, (r2 + h) % e_now * prior)
+                main = main + later
+            carry = incoming_x(w2, (r2 - h) % e_now * prior)
+            main = main + carry
+        return main
+
+    image_key_value = _state_wall(
+        cross_keyvalue_weight,
+        lambda own_block, start: jnp.einsum(
+            "ic,cjf->ijf",
+            lax.dynamic_slice_in_dim(image_norm, start, own_block.shape[0], axis=1),
+            own_block,
+            preferred_element_type=jnp.float32,
+        ),
     ).astype(jnp.bfloat16)
     earlier_tile = passed_along(image_key_value, "seq", 1)
     blocks = [(text_key_value, doc_ids)]

time: 131 us -> 128 us (0.977)
  waiting for transfers between devices: 43.2 us -> 34.3 us
  starting transfers between devices: 16 us -> 24.7 us
  local copies, waits for them, and re-layouts: 13.6 us -> 9.83 us
  matrix products: 22.5 us -> 23.9 us
    all_gather x1 -> x0, waiting for transfers between devices: 23.4 us -> none  [per_device(): lax.all_gather(cross_keyvalue_weight, 'seq', axis=0, tiled=True)]
    ppermute x0 -> x7, waiting for transfers between devices: none -> 12.9 us  [the longest x3 9.64 us: _state_wall(): x_new = lax.ppermute(x_new, axis_name='seq', perm=tray)]
    ppermute x0 -> x7, starting transfers between devices: none -> 9.56 us  [the longest x4 8.13 us: _state_wall(): w2 = lax.ppermute(w2, 'seq', nodes)]
    dot_general x1 -> x8, matrix products: 3.87 us -> 7.97 us  [per_device(): jnp.einsum('ic,cjf->ijf', lax.dynamic_slice_in_dim(image_norm, start, own...]
    dot_general x1, matrix products: 4.89 us -> 2.09 us  [per_device(): jnp.einsum('ycmq,qyb->mycb', self_attention_weights, all_keyval[1].reshap...]
    concatenate x1, other arithmetic: 2.08 us -> 0.07 us  [per_device(): image_all = jnp.concatenate([earlier_tile, image_key_value], axis=0)]
    ppermute x5, waiting for transfers between devices: 19.7 us -> 21.4 us  [passed_along(): return lax.ppermute(block, axis, route)]
    convert_element_type x0 -> x1, other arithmetic: none -> 1.5 us  [per_device(): image_norm = (mixed_sum * lax.rsqrt(jnp.mean(mixed_sum * mixed_sum, axis=...]
  transfers between devices with their start and end apart: 7 -> 13, of which waited for: 4 -> 6; matrix products, arithmetic and copies ran while one was open for 14% -> 23% of each run, Pallas kernels for 0% -> 0%
where the time goes in v1:
time: 128 us; the launch traced here: 126 us
  waiting for transfers between devices  34.3 us (27%)
  starting transfers between devices  24.7 us (19%)
  matrix products  23.9 us (19%)
  other arithmetic  19.6 us (15%)
  between operations  13.9 us (11%)
  local copies, waits for them, and re-layouts  9.83 us (8%)
    ppermute x5, waiting for transfers between devices, passed_along(): return lax.ppermute(block, axis, route)  21.4 us
    ppermute x5, starting transfers between devices, passed_along(): return lax.ppermute(block, axis, route)  15.2 us
    sub x2, other arithmetic, attend_heads(): return jax.nn.softmax(scores, axis=-1)  12.5 us
    ppermute x3, waiting for transfers between devices, _state_wall(): x_new = lax.ppermute(x_new, axis_name='seq', perm=tray)  9.64 us
    ppermute x4, starting transfers between devices, _state_wall(): w2 = lax.ppermute(w2, 'seq', nodes)  8.13 us
    dot_general x8, matrix products, per_device(): jnp.einsum('ic,cjf->ijf', lax.dynamic_slice_in_dim(image_norm, start, own...  7.97 us
    dot_general x2, matrix products, attend_heads(): jnp.einsum('tgrd,kgd->grtk', query_rows, keys, preferred_element_type=jnp...  5.54 us
    convert_element_type x1, other arithmetic, per_device(): (self_output + gate_cols[None, :] * cross_output).astype(jnp.bfloat16)  3.46 us
  transfers between devices with their start and end apart: 13, of which 6 were waited for; matrix products, arithmetic and copies ran while one was open for 23% of the time, Pallas kernels for 0%

profile of v1, /device:TPU:8, one launch (start us, length us, event | category | flops | bytes accessed | tf_op | source)
XLA Modules:
  0.0 126.3 jit_solution(17028116818884852207)
XLA Ops:
  6.5 1.1 copy.44
  7.7 1.4 %collective-permute-start.4 = (bf16[160,2,512]{2,0,1:T(8,128)(2,1)S(1)}, bf16[160,2,512]{2,0,1:T(8,128)(2,1)}, u32[]{:S(2)}, u32[]{:S(2)}) collective-permute-start(bf16[160,2,512]{2,0,1:T(8,128)(2,1)S(1)} %copy.44), channel_id=1, source_target_pairs={{0,14},{2,0},{4,2},{6,4},{8,6},{10,8},{12,10},{14,12},{1,15},{3,1}... | collective-permute-start | bytes 983048 | tf_op jit(solution)/shard_map/ppermute | solution.py:72
  9.1 0.6 collective-permute-start.5
  9.8 1.3 fusion.63
  11.0 0.2 copy.40
  11.2 0.2 copy.39
  11.4 0.2 copy.41
  11.6 2.2 %fusion.66 = (f32[8,256]{1,0:T(8,128)S(1)}, f32[8,256,256]{1,2,0:T(8,128)}) fusion(bf16[256,8,80]{0,2,1:T(8,128)(2,1)S(1)} %bitcast.115, bf16[256,8,80]{0,2,1:T(8,128)(2,1)S(1)} %bitcast.114), kind=kOutput, calls=%fused_computation.103 | convolution fusion | flops 85459200 | bytes 2760704 | tf_op jit(solution)/shard_map/sub | solution.py:49
  13.7 1.9 %convolution_convert_fusion = bf16[8,256,80]{1,2,0:T(8,128)(2,1)S(1)} fusion(bf16[256,8,80]{0,2,1:T(8,128)(2,1)S(1)} %bitcast.116, f32[8,256,256]{1,2,0:T(8,128)} %get-tuple-element.17, f32[8,256]{1,0:T(8,128)S(1)} %get-tuple-element.16), kind=kOutput, calls=%fused_computation.35 | convolution fusion | flops 85098496 | bytes 2760704 | tf_op jit(solution)/shard_map/hqk,khd->qhd/dot_general | solution.py:50
  15.7 1.9 %fusion.68 = f32[256,1280]{1,0:T(8,128)} fusion(bf16[256,640]{0,1:T(8,128)(2,1)S(1)} %bitcast.113, bf16[640,1280]{1,0:T(8,128)(2,1)S(1)} %copy-done), kind=kOutput, calls=%fused_computation.105 | convolution fusion | flops 419430400 | bytes 3276800 | tf_op jit(solution)/shard_map/dot_general | solution.py:54
  17.6 4.3 %collective-permute-start.2 = (s32[128]{0:T(128)S(1)}, s32[128]{0:T(128)S(1)}, u32[]{:S(2)}, u32[]{:S(2)}) collective-permute-start(s32[128]{0:T(128)S(1)} %copy-done.6), channel_id=1, source_target_pairs={{0,2},{2,4},{4,6},{6,8},{8,10},{10,12},{12,14},{1,3},{3,5},{5,7},{... | collective-permute-start | bytes 1544 | tf_op jit(solution)/shard_map/ppermute | solution.py:15
  21.9 0.2 copy.34
  22.1 2.6 %collective-permute-start = (bf16[2,128,512]{1,2,0:T(8,128)(2,1)S(1)}, bf16[2,128,512]{1,2,0:T(8,128)(2,1)S(1)}, u32[]{:S(2)}, u32[]{:S(2)}) collective-permute-start(bf16[2,128,512]{1,2,0:T(8,128)(2,1)S(1)} %copy.34), channel_id=1, source_target_pairs={{0,2},{2,4},{4,6},{6,8},{8,10},{10,12},{12,14},{1,3},{3,5},{5,7},{... | collective-permute-start | bytes 786440 | tf_op jit(solution)/shard_map/ppermute | solution.py:15
  24.9 0.1 compare_and_fusion
  25.1 0.2 copy.88
  25.3 4.3 %collective-permute-start.3 = (s32[128]{0:T(128)S(1)}, s32[128]{0:T(128)S(1)}, u32[]{:S(2)}, u32[]{:S(2)}) collective-permute-start(s32[128]{0:T(128)S(1)} %collective-permute-done.2), channel_id=1, source_target_pairs={{0,2},{2,4},{4,6},{6,8},{8,10},{10,12},{12,14},{1,3},{3,5},{5,7},{... | collective-permute-start | bytes 1544 | tf_op jit(solution)/shard_map/ppermute | solution.py:15
  29.7 2.4 %collective-permute-done = bf16[2,128,512]{1,2,0:T(8,128)(2,1)S(1)} collective-permute-done((bf16[2,128,512]{1,2,0:T(8,128)(2,1)S(1)}, bf16[2,128,512]{1,2,0:T(8,128)(2,1)S(1)}, u32[]{:S(2)}, u32[]{:S(2)}) %collective-permute-start) | collective-permute-done | bytes 262176 | tf_op jit(solution)/shard_map/ppermute | solution.py:15
  32.1 1.9 %collective-permute-start.1 = (bf16[2,128,512]{1,2,0:T(8,128)(2,1)S(1)}, bf16[2,128,512]{1,2,0:T(8,128)(2,1)S(1)}, u32[]{:S(2)}, u32[]{:S(2)}) collective-permute-start(bf16[2,128,512]{1,2,0:T(8,128)(2,1)S(1)} %collective-permute-done), channel_id=1, source_target_pairs={{0,2},{2,4},{4,6},{6,8},{8,10},{10,12},{12,14},{1,3},{3,5},{5,7},{... | collective-permute-start | bytes 786440 | tf_op jit(solution)/shard_map/ppermute | solution.py:15
  34.0 0.2 and_and_fusion
  34.3 3.1 %collective-permute-start.7 = (bf16[160,2,512]{2,0,1:T(8,128)(2,1)}, bf16[160,2,512]{2,0,1:T(8,128)(2,1)S(1)}, u32[]{:S(2)}, u32[]{:S(2)}) collective-permute-start(bf16[160,2,512]{2,0,1:T(8,128)(2,1)} %collective-permute-done.5), channel_id=1, source_target_pairs={{0,2},{2,4},{4,6},{6,8},{8,10},{10,12},{12,14},{14,0},{1,3},{3,5},... | collective-permute-start | bytes 983048 | tf_op jit(solution)/shard_map/ppermute | solution.py:70
  37.4 10.4 %collective-permute-done.1 = bf16[2,128,512]{1,2,0:T(8,128)(2,1)S(1)} collective-permute-done((bf16[2,128,512]{1,2,0:T(8,128)(2,1)S(1)}, bf16[2,128,512]{1,2,0:T(8,128)(2,1)S(1)}, u32[]{:S(2)}, u32[]{:S(2)}) %collective-permute-start.1) | collective-permute-done | bytes 262176 | tf_op jit(solution)/shard_map/ppermute | solution.py:15
  47.9 1.0 fusion.20
  49.0 3.2 %collective-permute-done.7 = bf16[160,2,512]{2,0,1:T(8,128)(2,1)S(1)} collective-permute-done((bf16[160,2,512]{2,0,1:T(8,128)(2,1)}, bf16[160,2,512]{2,0,1:T(8,128)(2,1)S(1)}, u32[]{:S(2)}, u32[]{:S(2)}) %collective-permute-start.7) | collective-permute-done | bytes 327712 | tf_op jit(solution)/shard_map/ppermute | solution.py:70
  52.2 2.4 %collective-permute-start.9 = (bf16[160,2,512]{2,0,1:T(8,128)(2,1)S(1)}, bf16[160,2,512]{2,0,1:T(8,128)(2,1)}, u32[]{:S(2)}, u32[]{:S(2)}) collective-permute-start(bf16[160,2,512]{2,0,1:T(8,128)(2,1)S(1)} %collective-permute-done.7), channel_id=1, source_target_pairs={{0,2},{2,4},{4,6},{6,8},{8,10},{10,12},{12,14},{14,0},{1,3},{3,5},... | collective-permute-start | bytes 983048 | tf_op jit(solution)/shard_map/ppermute | solution.py:70
  54.6 3.6 %fusion.65 = (f32[4,8,128]{2,1,0:T(8,128)S(1)}, f32[4,8,128,384]{2,3,1,0:T(8,128)}) fusion(f32[4,384,128,8]{2,1,3,0:T(8,128)S(1)} %fusion.20, pred[128,384]{0,1:T(8,128)(4,1)S(1)} %and_and_fusion), kind=kOutput, calls=%fused_computation.102 | output fusion | flops 9437567 | bytes 12648448 | tf_op jit(solution)/shard_map/sub | solution.py:23
  58.2 4.1 %collective-permute-done.6 = bf16[160,2,512]{2,0,1:T(8,128)(2,1)} collective-permute-done((bf16[160,2,512]{2,0,1:T(8,128)(2,1)}, bf16[160,2,512]{2,0,1:T(8,128)(2,1)}, u32[]{:S(2)}, u32[]{:S(2)}) %collective-permute-start.6) | collective-permute-done | bytes 327712 | tf_op jit(solution)/shard_map/ppermute | solution.py:72
  62.3 2.0 %collective-permute-start.10 = (bf16[160,2,512]{2,0,1:T(8,128)(2,1)}, bf16[160,2,512]{2,0,1:T(8,128)(2,1)S(1)}, u32[]{:S(2)}, u32[]{:S(2)}) collective-permute-start(bf16[160,2,512]{2,0,1:T(8,128)(2,1)} %collective-permute-done.9), channel_id=1, source_target_pairs={{0,2},{2,4},{4,6},{6,8},{8,10},{10,12},{12,14},{14,0},{1,3},{3,5},... | collective-permute-start | bytes 983048 | tf_op jit(solution)/shard_map/ppermute | solution.py:70
  64.4 1.6 %multiply_reduce_fusion.1 = f32[256]{0:T(256)S(1)} fusion(f32[256,1280]{1,0:T(8,128)} %all-reduce.2.cloned.1.call-done, bf16[256,1280]{1,0:T(8,128)(2,1)S(1)} %copy-done.2), kind=kLoop, calls=%fused_computation.32 | loop fusion | flops 1310464 | bytes 1967104 | tf_op jit(solution)/shard_map/reduce_sum | solution.py:57
  65.9 1.5 %multiply_convert_fusion.2 = bf16[256,1280]{1,0:T(8,128)(2,1)S(1)} fusion(f32[256,1280]{1,0:T(8,128)} %all-reduce.2.cloned.1.call-done, bf16[256,1280]{1,0:T(8,128)(2,1)S(1)} %copy-done.2, f32[256]{0:T(256)S(1)} %add_rsqrt_fusion), kind=kLoop, calls=%fused_computation.31 | loop fusion | flops 1310720 | bytes 2622464 | tf_op jit(solution)/shard_map/convert_element_type | solution.py:58
  67.5 0.4 fusion.35
  67.8 0.3 fusion.30
  68.2 1.5 %convolution_add_fusion.4 = f32[256,2,512]{2,0,1:T(8,128)S(1)} fusion(f32[256,2,512]{2,0,1:T(8,128)S(1)} %fusion.35, bf16[160,2,512]{2,0,1:T(8,128)(2,1)} %collective-permute-done.4, bf16[256,1280]{1,0:T(8,128)(2,1)S(1)} %multiply_convert_fusion.2, s32[]{:T(128)S(6)} %select_n.75), kind=kOutput, calls=%fused_computation.30 | convolution fusion | flops 84148224 | bytes 2555908 | tf_op jit(solution)/shard_map/ic,cjf->ijf/dot_general | solution.py:81
  69.7 1.3 %convolution_add_fusion.3 = f32[256,2,512]{2,0,1:T(8,128)S(1)} fusion(f32[256,2,512]{2,0,1:T(8,128)S(1)} %convolution_add_fusion.4, bf16[160,2,512]{2,0,1:T(8,128)(2,1)} %collective-permute-done.5, bf16[256,1280]{1,0:T(8,128)(2,1)S(1)} %multiply_convert_fusion.2, s32[]{:T(128)S(6)} %select_n.77), kind=kOutput, calls=%fused_computation.29 | convolution fusion | flops 84148224 | bytes 2555908 | tf_op jit(solution)/shard_map/ic,cjf->ijf/dot_general | solution.py:81
  71.0 1.5 %fusion.15 = f32[256,2,512]{2,0,1:T(8,128)S(1)} fusion(f32[256,2,512]{2,0,1:T(8,128)S(1)} %fusion.30, f32[256,2,512]{2,0,1:T(8,128)S(1)} %convolution_add_fusion.3, bf16[160,2,512]{2,0,1:T(8,128)(2,1)} %collective-permute-done.6, bf16[256,1280]{1,0:T(8,128)(2,1)S(1)} %multiply_convert_fusion.2, s32[]{:T(128)S(6)} %select_n.79), kind=kOutput, calls=%fused_computation.28 | convolution fusion | flops 84410368 | bytes 3604484 | tf_op jit(solution)/shard_map/ic,cjf->ijf/dot_general | solution.py:81
  72.5 1.3 %fusion.27 = f32[256,2,512]{2,0,1:T(8,128)S(1)} fusion(bf16[160,2,512]{2,0,1:T(8,128)(2,1)} %collective-permute-done.9, bf16[256,1280]{1,0:T(8,128)(2,1)S(1)} %multiply_convert_fusion.2, s32[]{:T(128)S(6)} %select_n.85), kind=kOutput, calls=%fused_computation.51 | convolution fusion | flops 83886080 | bytes 1507332 | tf_op jit(solution)/shard_map/ic,cjf->ijf/dot_general | solution.py:81
  73.8 5.5 %collective-permute-done.8 = bf16[160,2,512]{2,0,1:T(8,128)(2,1)} collective-permute-done((bf16[160,2,512]{2,0,1:T(8,128)(2,1)}, bf16[160,2,512]{2,0,1:T(8,128)(2,1)}, u32[]{:S(2)}, u32[]{:S(2)}) %collective-permute-start.8) | collective-permute-done | bytes 327712 | tf_op jit(solution)/shard_map/ppermute | solution.py:72
  79.3 1.3 %fusion.14 = f32[256,2,512]{2,0,1:T(8,128)S(1)} fusion(f32[256,2,512]{2,0,1:T(8,128)S(1)} %fusion.27, f32[256,2,512]{2,0,1:T(8,128)S(1)} %fusion.15, bf16[160,2,512]{2,0,1:T(8,128)(2,1)} %collective-permute-done.8, bf16[256,1280]{1,0:T(8,128)(2,1)S(1)} %multiply_convert_fusion.2, s32[]{:T(128)S(6)} %select_n.83), kind=kOutput, calls=%fused_computation.26 | convolution fusion | flops 84410368 | bytes 3604484 | tf_op jit(solution)/shard_map/ic,cjf->ijf/dot_general | solution.py:81
  80.7 0.4 fusion.16
  81.0 2.1 %collective-permute-start.11 = (bf16[256,2,512]{2,0,1:T(8,128)(2,1)S(1)}, bf16[256,2,512]{2,0,1:T(8,128)(2,1)S(1)}, u32[]{:S(2)}, u32[]{:S(2)}) collective-permute-start(bf16[256,2,512]{2,0,1:T(8,128)(2,1)S(1)} %fusion.16), channel_id=1, source_target_pairs={{0,2},{2,4},{4,6},{6,8},{8,10},{10,12},{12,14},{1,3},{3,5},{5,7},{... | collective-permute-start | bytes 1572872 | tf_op jit(solution)/shard_map/ppermute | solution.py:15
  83.1 2.1 %fusion.11 = f32[4,128,8,128]{3,1,2,0:T(8,128)} fusion(bf16[384,4,128,1]{0,2,3,1:T(8,128)(2,1)S(1)} %bitcast.112, f32[4,8,128,384]{2,3,1,0:T(8,128)S(1)} %bitcast.118, f32[4,8,128]{2,1,0:T(8,128)S(1)} %get-tuple-element.14), kind=kOutput, calls=%fused_computation.17 | convolution fusion | flops 405798912 | bytes 8798208 | tf_op jit(solution)/shard_map/ycmq,qyb->mycb/dot_general | solution.py:109
  85.2 2.9 %copy.59 = f32[128,4096]{1,0:T(8,128)} copy(f32[128,4096]{0,1:T(8,128)} %bitcast.108) | data formatting | bytes 4194304 | tf_op jit(solution)/shard_map/reshape | solution.py:115
  88.2 8.6 %collective-permute-done.11 = bf16[256,2,512]{2,0,1:T(8,128)(2,1)S(1)} collective-permute-done((bf16[256,2,512]{2,0,1:T(8,128)(2,1)S(1)}, bf16[256,2,512]{2,0,1:T(8,128)(2,1)S(1)}, u32[]{:S(2)}, u32[]{:S(2)}) %collective-permute-start.11) | collective-permute-done | bytes 524320 | tf_op jit(solution)/shard_map/ppermute | solution.py:15
  97.0 4.5 %fusion.18 = f32[4,512,128,8]{2,1,3,0:T(8,128)} fusion(bf16[128,4,8,128]{3,2,1,0:T(8,128)(2,1)S(1)} %bitcast.105, bf16[512,4,128,1]{2,1,0,3:T(4,128)(2,1)S(1)} %bitcast.106), kind=kOutput, calls=%fused_computation.39 | convolution fusion | flops 536870912 | bytes 9961472 | tf_op jit(solution)/shard_map/tgrd,kgd->grtk/dot_general | solution.py:19
  101.5 0.2 copy.85
  101.7 8.9 %fusion.67 = (f32[4,8,128]{2,1,0:T(8,128)S(1)}, f32[4,8,128,512]{2,3,1,0:T(8,128)S(1)}) fusion(f32[4,512,128,8]{2,1,3,0:T(8,128)} %fusion.18, pred[128,512]{0,1:T(8,128)(4,1)S(1)} %compare_and_fusion), kind=kOutput, calls=%fused_computation.104 | output fusion | flops 12583423 | bytes 16859136 | tf_op jit(solution)/shard_map/sub | solution.py:23
  110.6 2.3 %fusion.8 = f32[4,128,8,128]{3,1,2,0:T(8,128)} fusion(bf16[512,4,128,1]{0,2,3,1:T(8,128)(2,1)S(1)} %bitcast.111, f32[4,8,128,512]{2,3,1,0:T(8,128)S(1)} %get-tuple-element.19, f32[128]{0:T(128)S(1)} %compare_convert_fusion, f32[4,8,128]{2,1,0:T(8,128)S(1)} %get-tuple-element.18), kind=kOutput, calls=%fused_computation.14 | convolution fusion | flops 543162368 | bytes 11026944 | tf_op jit(solution)/shard_map/ycmq,qyb->mycb/dot_general | solution.py:129
  113.0 3.0 %copy.58 = f32[128,4096]{1,0:T(8,128)} copy(f32[128,4096]{0,1:T(8,128)} %bitcast.107) | data formatting | bytes 4194304 | tf_op jit(solution)/shard_map/reshape | solution.py:135
  116.0 3.5 %add_convert_fusion = bf16[128,4096]{1,0:T(8,128)(2,1)} fusion(f32[128,4096]{1,0:T(8,128)} %copy.59, f32[128,4096]{1,0:T(8,128)} %copy.58, f32[4096]{0:T(1024)S(1)} %broadcast_bitcast_fusion), kind=kLoop, calls=%fused_computation.19 | loop fusion | flops 1572864 | bytes 5259264 | tf_op jit(solution)/shard_map/convert_element_type | solution.py:137
  (48 shorter events, 0.6 us)
Async XLA Ops:
  6.5 9.2 %copy-start = (bf16[640,1280]{1,0:T(8,128)(2,1)S(1)}, bf16[640,1280]{1,0:T(8,128)(2,1)}, u32[]{:S(2)}) copy-start(bf16[640,1280]{1,0:T(8,128)(2,1)} %param.15) | copy-start | bytes 4915204
  6.5 57.8 %all-reduce.2.cloned.1.call-start = ((), (), s32[]{:S(2)}) async-start(), calls=%async_computation | async-start | bytes 2621440 | tf_op jit(solution)/shard_map/psum | solution.py:55
  7.7 29.7 %collective-permute-start.4 = (bf16[160,2,512]{2,0,1:T(8,128)(2,1)S(1)}, bf16[160,2,512]{2,0,1:T(8,128)(2,1)}, u32[]{:S(2)}, u32[]{:S(2)}) collective-permute-start(bf16[160,2,512]{2,0,1:T(8,128)(2,1)S(1)} %copy.44), channel_id=1, source_target_pairs={{0,14},{2,0},{4,2},{6,4},{8,6},{10,8},{12,10},{14,12},{1,15},{3,1}... | collective-permute-start | bytes 983048 | tf_op jit(solution)/shard_map/ppermute | solution.py:72
  9.1 25.2 %collective-permute-start.5 = (bf16[160,2,512]{2,0,1:T(8,128)(2,1)S(1)}, bf16[160,2,512]{2,0,1:T(8,128)(2,1)}, u32[]{:S(2)}, u32[]{:S(2)}) collective-permute-start(bf16[160,2,512]{2,0,1:T(8,128)(2,1)S(1)} %copy.44), channel_id=1, source_target_pairs={{0,2},{2,4},{4,6},{6,8},{8,10},{10,12},{12,14},{14,0},{1,3},{3,5},... | collective-permute-start | bytes 983048 | tf_op jit(solution)/shard_map/ppermute | solution.py:70
  15.6 2.0 %copy-start.6 = (s32[128]{0:T(128)S(1)}, s32[128]{0:T(128)}, u32[]{:S(2)}) copy-start(s32[128]{0:T(128)} %param.11) | copy-start | bytes 1540
  15.6 6.3 %copy-start.5 = (bf16[2,128,512]{2,1,0:T(8,128)(2,1)S(1)}, bf16[2,128,512]{2,1,0:T(8,128)(2,1)}, u32[]{:S(2)}) copy-start(bf16[2,128,512]{2,1,0:T(8,128)(2,1)} %param.10) | copy-start | bytes 786436
  15.6 9.0 %copy-start.7 = (s32[128,2]{0,1:T(2,128)S(1)}, s32[128,2]{0,1:T(2,128)}, u32[]{:S(2)}) copy-start(s32[128,2]{0,1:T(2,128)} %param.12) | copy-start | bytes 3076
  15.7 9.1 %copy-start.8 = (f32[32]{0:T(128)S(1)}, f32[32]{0:T(128)}, u32[]{:S(2)}) copy-start(f32[32]{0:T(128)} %param.17) | copy-start | bytes 388
  15.7 9.4 %copy-start.4 = (bf16[128,4096]{1,0:T(8,128)(2,1)S(1)}, bf16[128,4096]{1,0:T(8,128)(2,1)}, u32[]{:S(2)}) copy-start(bf16[128,4096]{1,0:T(8,128)(2,1)} %param.9) | copy-start | bytes 3145732
  17.6 7.7 %collective-permute-start.2 = (s32[128]{0:T(128)S(1)}, s32[128]{0:T(128)S(1)}, u32[]{:S(2)}, u32[]{:S(2)}) collective-permute-start(s32[128]{0:T(128)S(1)} %copy-done.6), channel_id=1, source_target_pairs={{0,2},{2,4},{4,6},{6,8},{8,10},{10,12},{12,14},{1,3},{3,5},{5,7},{... | collective-permute-start | bytes 1544 | tf_op jit(solution)/shard_map/ppermute | solution.py:15
  22.1 10.0 %collective-permute-start = (bf16[2,128,512]{1,2,0:T(8,128)(2,1)S(1)}, bf16[2,128,512]{1,2,0:T(8,128)(2,1)S(1)}, u32[]{:S(2)}, u32[]{:S(2)}) collective-permute-start(bf16[2,128,512]{1,2,0:T(8,128)(2,1)S(1)} %copy.34), channel_id=1, source_target_pairs={{0,2},{2,4},{4,6},{6,8},{8,10},{10,12},{12,14},{1,3},{3,5},{5,7},{... | collective-permute-start | bytes 786440 | tf_op jit(solution)/shard_map/ppermute | solution.py:15
  25.3 8.7 %collective-permute-start.3 = (s32[128]{0:T(128)S(1)}, s32[128]{0:T(128)S(1)}, u32[]{:S(2)}, u32[]{:S(2)}) collective-permute-start(s32[128]{0:T(128)S(1)} %collective-permute-done.2), channel_id=1, source_target_pairs={{0,2},{2,4},{4,6},{6,8},{8,10},{10,12},{12,14},{1,3},{3,5},{5,7},{... | collective-permute-start | bytes 1544 | tf_op jit(solution)/shard_map/ppermute | solution.py:15
  32.1 15.6 %collective-permute-start.1 = (bf16[2,128,512]{1,2,0:T(8,128)(2,1)S(1)}, bf16[2,128,512]{1,2,0:T(8,128)(2,1)S(1)}, u32[]{:S(2)}, u32[]{:S(2)}) collective-permute-start(bf16[2,128,512]{1,2,0:T(8,128)(2,1)S(1)} %collective-permute-done), channel_id=1, source_target_pairs={{0,2},{2,4},{4,6},{6,8},{8,10},{10,12},{12,14},{1,3},{3,5},{5,7},{... | collective-permute-start | bytes 786440 | tf_op jit(solution)/shard_map/ppermute | solution.py:15
  34.3 17.9 %collective-permute-start.7 = (bf16[160,2,512]{2,0,1:T(8,128)(2,1)}, bf16[160,2,512]{2,0,1:T(8,128)(2,1)S(1)}, u32[]{:S(2)}, u32[]{:S(2)}) collective-permute-start(bf16[160,2,512]{2,0,1:T(8,128)(2,1)} %collective-permute-done.5), channel_id=1, source_target_pairs={{0,2},{2,4},{4,6},{6,8},{8,10},{10,12},{12,14},{14,0},{1,3},{3,5},... | collective-permute-start | bytes 983048 | tf_op jit(solution)/shard_map/ppermute | solution.py:70
  37.4 25.0 %collective-permute-start.6 = (bf16[160,2,512]{2,0,1:T(8,128)(2,1)}, bf16[160,2,512]{2,0,1:T(8,128)(2,1)}, u32[]{:S(2)}, u32[]{:S(2)}) collective-permute-start(bf16[160,2,512]{2,0,1:T(8,128)(2,1)} %collective-permute-done.4), channel_id=1, source_target_pairs={{0,14},{2,0},{4,2},{6,4},{8,6},{10,8},{12,10},{14,12},{1,15},{3,1}... | collective-permute-start | bytes 983048 | tf_op jit(solution)/shard_map/ppermute | solution.py:72
  49.0 15.4 %copy-start.2 = (bf16[256,1280]{1,0:T(8,128)(2,1)S(1)}, bf16[256,1280]{1,0:T(8,128)(2,1)}, u32[]{:S(2)}) copy-start(bf16[256,1280]{1,0:T(8,128)(2,1)} %param.13) | copy-start | bytes 1966084
  52.2 10.1 %collective-permute-start.9 = (bf16[160,2,512]{2,0,1:T(8,128)(2,1)S(1)}, bf16[160,2,512]{2,0,1:T(8,128)(2,1)}, u32[]{:S(2)}, u32[]{:S(2)}) collective-permute-start(bf16[160,2,512]{2,0,1:T(8,128)(2,1)S(1)} %collective-permute-done.7), channel_id=1, source_target_pairs={{0,2},{2,4},{4,6},{6,8},{8,10},{10,12},{12,14},{14,0},{1,3},{3,5},... | collective-permute-start | bytes 983048 | tf_op jit(solution)/shard_map/ppermute | solution.py:70
  58.2 9.3 %copy-start.3 = (bf16[160,2,512]{2,1,0:T(2,128)(2,1)S(1)}, bf16[160,2,512]{2,1,0:T(2,128)(2,1)}, u32[]{:S(2)}) copy-start(bf16[160,2,512]{2,1,0:T(2,128)(2,1)} %param.16) | copy-start | bytes 983044
  62.3 17.0 %collective-permute-start.8 = (bf16[160,2,512]{2,0,1:T(8,128)(2,1)}, bf16[160,2,512]{2,0,1:T(8,128)(2,1)}, u32[]{:S(2)}, u32[]{:S(2)}) collective-permute-start(bf16[160,2,512]{2,0,1:T(8,128)(2,1)} %collective-permute-done.6), channel_id=1, source_target_pairs={{0,14},{2,0},{4,2},{6,4},{8,6},{10,8},{12,10},{14,12},{1,15},{3,1}... | collective-permute-start | bytes 983048 | tf_op jit(solution)/shard_map/ppermute | solution.py:72
  62.3 18.3 %collective-permute-start.10 = (bf16[160,2,512]{2,0,1:T(8,128)(2,1)}, bf16[160,2,512]{2,0,1:T(8,128)(2,1)S(1)}, u32[]{:S(2)}, u32[]{:S(2)}) collective-permute-start(bf16[160,2,512]{2,0,1:T(8,128)(2,1)} %collective-permute-done.9), channel_id=1, source_target_pairs={{0,2},{2,4},{4,6},{6,8},{8,10},{10,12},{12,14},{14,0},{1,3},{3,5},... | collective-permute-start | bytes 983048 | tf_op jit(solution)/shard_map/ppermute | solution.py:70
  68.2 14.9 %slice-start = ((s8[6291456]{0:T(1024)(128)(4,1)}), s8[4194304]{0:T(1024)(128)(4,1)S(1)}, s32[]{:S(2)}) async-start(s8[6291456]{0:T(1024)(128)(4,1)} %bitcast.117), calls=%async_computation.1 | async-start | bytes 8388608
  71.0 12.1 %slice-start.1 = ((s8[6291456]{0:T(1024)(128)(4,1)}), s8[2097152]{0:T(1024)(128)(4,1)S(1)}, s32[]{:S(2)}) async-start(s8[6291456]{0:T(1024)(128)(4,1)} %bitcast.117), calls=%async_computation.2 | async-start | bytes 4194304
  81.0 15.8 %collective-permute-start.11 = (bf16[256,2,512]{2,0,1:T(8,128)(2,1)S(1)}, bf16[256,2,512]{2,0,1:T(8,128)(2,1)S(1)}, u32[]{:S(2)}, u32[]{:S(2)}) collective-permute-start(bf16[256,2,512]{2,0,1:T(8,128)(2,1)S(1)} %fusion.16), channel_id=1, source_target_pairs={{0,2},{2,4},{4,6},{6,8},{8,10},{10,12},{12,14},{1,3},{3,5},{5,7},{... | collective-permute-start | bytes 1572872 | tf_op jit(solution)/shard_map/ppermute | solution.py:15
  113.0 6.5 %copy-start.1 = (bf16[640,1280]{1,0:T(8,128)(2,1)S(1)}, bf16[640,1280]{1,0:T(8,128)(2,1)}, u32[]{:S(2)}) copy-start(bf16[640,1280]{1,0:T(8,128)(2,1)} %param.15) | copy-start | bytes 4915204
Sparse Core Ops, SparseCore 0:
  17.7 24.1 all-reduce.1
